TPU v7x, 32 devices: a whole 2x2x4 slice. The times are simulated.
32 devices in a mesh: plane: 16 (over z, y, core), depth: 2 (over x).
Axes of the slice: x: 2, y: 2, z: 4, core: 2. Of those that a mesh axis runs over, the one named last changes fastest.
Arguments:
- volume: float32 [64, 512, 256], P('plane', None, 'depth'), may hold values from -6 to 6
- resample: bfloat16 [512, 512], replicated, may hold values from 0 to 1, as said below
- transfer: float32 [16, 4], replicated, may hold values from 0.2 to 2
- light: float32 [3], replicated, may hold values from -4 to 4
- ray_bounds: int32 [2, 64, 512], replicated, may hold values from 0 to 256, as said below
Outputs:
- frame: float32 [4, 64, 512], P(None, 'plane', 'depth')
Inputs may be any that keep to these rules, and one draw needn't show every extreme that they name: ray_bounds[0] < ray_bounds[1] for every pixel. `resample`: row v has nonzero entries only in columns v - 1, v and v + 1.
All inputs are finite; a program needn't handle non-finite values.
Results may differ from a plain program's by a relative error of at most 0.0003.
Values sent between devices are 32-bit elements; how exact they have to be, the bound alone decides.
A program may use at most 64 MiB of HBM per device.

v0:
```python
import jax
import jax.numpy as jnp
from jax import lax
from jax.sharding import PartitionSpec as P


def extended(block, sides, width):
    for axis, dim in sides:
        count = lax.axis_size(axis)
        forward = [(i, i + 1) for i in range(count - 1)]
        backward = [(target, source) for source, target in forward]
        low = lax.ppermute(
            lax.slice_in_dim(block, block.shape[dim] - width, None, axis=dim), axis, forward
        )
        high = lax.ppermute(lax.slice_in_dim(block, 0, width, axis=dim), axis, backward)
        block = jnp.concatenate([low, block, high], axis=dim)
    return block


def passed_along(value, axis, steps):
    count = lax.axis_size(axis)
    first, last = (max(0, -steps), min(count, count - steps))
    return lax.ppermute(value, axis, [(source, source + steps) for source in range(first, last)])


def shade(density, grad_x, grad_y, grad_z, transfer, light):
    scaled = jnp.clip((density + 2.5) / 5.0, 0.0, 1.0) * (transfer.shape[0] - 1)
    sigma = jnp.zeros_like(density)
    red = jnp.zeros_like(density)
    green = jnp.zeros_like(density)
    blue = jnp.zeros_like(density)
    for knot in range(transfer.shape[0]):
        hat = jnp.maximum(0.0, 1.0 - jnp.abs(scaled - knot))
        sigma = sigma + hat * transfer[knot, 3]
        red = red + hat * transfer[knot, 0]
        green = green + hat * transfer[knot, 1]
        blue = blue + hat * transfer[knot, 2]
    lit = jnp.abs(grad_x * light[0] + grad_y * light[1] + grad_z * light[2])
    lit = 0.3 + 0.7 * lit / jnp.sqrt(grad_x * grad_x + grad_y * grad_y + grad_z * grad_z + 1.0)
    return (sigma, red * lit, green * lit, blue * lit)


def over(front, back):
    return jnp.concatenate([front[:3] + front[3:] * back[:3], front[3:] * back[3:]], axis=0)


def blank_like(piece):
    return jnp.concatenate([jnp.zeros_like(piece[:3]), jnp.ones_like(piece[3:])], axis=0)


def fold_pieces(pieces):
    result = pieces[0]
    for piece in pieces[1:]:
        result = over(result, piece)
    return jnp.concatenate([result[:3], 1.0 - result[3:]], axis=0)


def body(volume, resample, transfer, light, ray_bounds):
    cells_x, cells_y, cells_z = volume.shape
    planes = lax.axis_size("plane")
    depths = lax.axis_size("depth")
    plane_index = lax.axis_index("plane")
    depth_index = lax.axis_index("depth")
    padded = extended(volume, (("plane", 0), ("depth", 2)), 1)
    grad_x = (padded[2:, :, 1:-1] - padded[:-2, :, 1:-1]) * 0.5
    grad_z = (padded[1:-1, :, 2:] - padded[1:-1, :, :-2]) * 0.5
    side_pad = jnp.pad(volume, ((0, 0), (1, 1), (0, 0)))
    grad_y = (side_pad[:, 2:] - side_pad[:, :-2]) * 0.5
    fields = jnp.stack(
        [
            volume.astype(jnp.bfloat16),
            grad_x.astype(jnp.bfloat16),
            grad_y.astype(jnp.bfloat16),
            grad_z.astype(jnp.bfloat16),
        ]
    )
    samples = lax.dot_general(
        resample, fields, (((1,), (2,)), ((), ())), preferred_element_type=jnp.float32
    )
    sigma, red, green, blue = shade(
        samples[:, 0], samples[:, 1], samples[:, 2], samples[:, 3], transfer, light
    )
    channels = jnp.stack([sigma, red, green, blue])
    group = cells_z // cells_x
    shifted = []
    for offset in range(cells_x):
        piece = channels[:, :, :, offset * group : (offset + 1) * group]
        shifted.append(jnp.pad(piece, ((0, 0), (0, 0), (offset, cells_x - offset), (0, 0))))
    sheared = jnp.concatenate(shifted, axis=3)
    column_block = plane_index + depth_index

    def bound_rows(block):
        start = jnp.minimum(block, planes - 1) * cells_x
        return lax.dynamic_slice_in_dim(ray_bounds, start, cells_x, 1)

    bounds_here = jnp.concatenate([bound_rows(column_block), bound_rows(column_block + 1)], axis=1)
    bounds_here = bounds_here.transpose(0, 2, 1)
    sample_index = depth_index * cells_z + jnp.arange(cells_z, dtype=jnp.int32)
    inside = (sample_index >= bounds_here[0][:, :, None]) & (
        sample_index < bounds_here[1][:, :, None]
    )
    step_size = 2.0 / (depths * cells_z)
    tau = step_size * sheared[0] * inside.astype(jnp.float32)
    earlier = (jnp.arange(cells_z)[:, None] < jnp.arange(cells_z)[None, :]).astype(jnp.float32)
    before = jnp.dot(tau.reshape(-1, cells_z), earlier, precision=lax.Precision.HIGHEST).reshape(
        tau.shape
    )
    weight = jnp.exp(-before) * (1.0 - jnp.exp(-tau))
    color = jnp.sum(weight[None] * sheared[1:], axis=3)
    remain = jnp.exp(-jnp.sum(tau, axis=2))
    partial_value = jnp.concatenate([color, remain[None]], axis=0).transpose(0, 2, 1)
    lower = partial_value[:, :cells_x]
    upper = partial_value[:, cells_x:]
    upper_prev = passed_along(upper, "plane", 1)
    upper_prev = jnp.where(plane_index == 0, blank_like(upper_prev), upper_prev)
    merged = over(lower, upper_prev)
    bit_count = (depths - 1).bit_length()
    row_share = cells_y // depths
    aligned = merged
    for bit_number in range(bit_count):
        moved = passed_along(aligned, "plane", 1 << bit_number)
        aligned = jnp.where(jnp.right_shift(depth_index, bit_number) % 2 == 1, moved, aligned)
    aligned = jnp.where(plane_index < depth_index, blank_like(aligned), aligned)
    gathered = lax.all_gather(aligned[None], "depth", axis=0, tiled=True)
    whole = fold_pieces([gathered[member] for member in range(depths)])
    return lax.dynamic_slice_in_dim(whole, depth_index * row_share, row_share, 2)


def solution(mesh):
    in_specs = (P("plane", None, "depth"), P(), P(), P(), P())
    out_specs = P(None, "plane", "depth")
    return jax.shard_map(body, mesh=mesh, in_specs=in_specs, out_specs=out_specs, check_vma=False)
```

profile of v0, /device:TPU:16, one launch (start us, length us, event | category | flops | bytes accessed | tf_op | source)
XLA Modules:
  0.0 102.8 jit_solution(12180218707748528670)
XLA Ops:
  0.0 1.6 %copy.15 = f32[4,512,128]{1,2,0:T(8,128)S(1)} copy(f32[4,512,128]{2,1,0:T(8,128)} %param.5) | data formatting | bytes 2097152 | tf_op args[0]
  1.7 2.8 %collective-permute-start = (f32[1,512,128]{1,2,0:T(8,128)S(1)}, f32[1,512,128]{1,2,0:T(8,128)S(1)}, u32[]{:S(2)}, u32[]{:S(2)}) collective-permute-start(f32[1,512,128]{1,2,0:T(8,128)S(1)} %get-tuple-element.18), channel_id=1, source_target_pairs={{2,0},{4,2},{6,4},{8,6},{10,8},{12,10},{14,12},{16,14},{18,16},{20... | collective-permute-start | bytes 786440 | tf_op jit(solution)/shard_map/ppermute | solution.py:15
  4.4 1.9 %collective-permute-start.1 = (f32[1,512,128]{1,2,0:T(8,128)S(1)}, f32[1,512,128]{1,2,0:T(8,128)S(1)}, u32[]{:S(2)}, u32[]{:S(2)}) collective-permute-start(f32[1,512,128]{1,2,0:T(8,128)S(1)} %get-tuple-element.17), channel_id=1, source_target_pairs={{0,2},{2,4},{4,6},{6,8},{8,10},{10,12},{12,14},{14,16},{16,18},{18... | collective-permute-start | bytes 786440 | tf_op jit(solution)/shard_map/ppermute | solution.py:12
  7.1 0.7 fusion.51
  7.8 0.7 fusion.50
  9.2 0.8 constant_dynamic-slice_fusion.1
  10.7 2.3 %collective-permute-done.1 = f32[1,512,128]{1,2,0:T(8,128)S(1)} collective-permute-done((f32[1,512,128]{1,2,0:T(8,128)S(1)}, f32[1,512,128]{1,2,0:T(8,128)S(1)}, u32[]{:S(2)}, u32[]{:S(2)}) %collective-permute-start.1) | collective-permute-done | bytes 262176 | tf_op jit(solution)/shard_map/ppermute | solution.py:12
  13.1 1.3 %collective-permute-start.2 = (f32[6,512,1]{1,2,0:T(1,128)S(1)}, f32[6,512,1]{1,2,0:T(1,128)S(1)}, u32[]{:S(2)}, u32[]{:S(2)}) collective-permute-start(f32[6,512,1]{1,2,0:T(1,128)S(1)} %get-tuple-element.13), channel_id=1, source_target_pairs={{1,0},{3,2},{5,4},{7,6},{9,8},{11,10},{13,12},{15,14},{17,16},{19,... | collective-permute-start | bytes 36872 | tf_op jit(solution)/shard_map/ppermute | solution.py:15
  14.3 4.5 %collective-permute-start.3 = (f32[6,512,1]{1,2,0:T(1,128)S(1)}, f32[6,512,1]{1,2,0:T(1,128)S(1)}, u32[]{:S(2)}, u32[]{:S(2)}) collective-permute-start(f32[6,512,1]{1,2,0:T(1,128)S(1)} %get-tuple-element.14), channel_id=1, source_target_pairs={{0,1},{2,3},{4,5},{6,7},{8,9},{10,11},{12,13},{14,15},{16,17},{18,... | collective-permute-start | bytes 36872 | tf_op jit(solution)/shard_map/ppermute | solution.py:12
  18.9 1.4 %collective-permute-done.3 = f32[6,512,1]{1,2,0:T(1,128)S(1)} collective-permute-done((f32[6,512,1]{1,2,0:T(1,128)S(1)}, f32[6,512,1]{1,2,0:T(1,128)S(1)}, u32[]{:S(2)}, u32[]{:S(2)}) %collective-permute-start.3) | collective-permute-done | bytes 12320 | tf_op jit(solution)/shard_map/ppermute | solution.py:12
  20.3 0.9 fusion.33
  21.2 1.3 %convolution_bitcast_fusion = f32[512,4,4,128]{0,3,2,1:T(8,128)S(1)} fusion(bf16[1,4,512,128]{2,3,1,0:T(8,128)(2,1)S(1)} %get-tuple-element.12, bf16[1,4,512,128]{2,3,1,0:T(8,128)(2,1)S(1)} %get-tuple-element.16, bf16[1,4,512,128]{2,3,1,0:T(8,128)(2,1)S(1)} %get-tuple-element.11, bf16[1,4,512,128]{2,3,1,0:T(8,128)(2,1)S(1)} %get-tuple-element.15, ...), kind=kOutput, calls=%fused_computation.14 | convolution fusion | flops 1076887552 | bytes 6815744 | tf_op jit(solution)/shard_map/dot_general | solution.py:77
  22.5 15.7 %bitcast_multiply_fusion = (f32[1,512,4,128]{1,3,2,0:T(8,128)S(1)}, f32[512,1,4,128]{0,3,2,1:T(8,128)S(1)}) fusion(f32[]{:T(128)} %bitcast.58, f32[]{:T(128)} %bitcast.56, f32[]{:T(128)} %bitcast.54, f32[]{:T(128)} %bitcast.52, f32[]{:T(128)} %bitcast.50, f32[]{:T(128)} %bitcast.48, f32[]{:T(128)} %bitcast.46, f32[]{:T(128)} %bitcast.44, f32[]{:T(128)} %bitcast.42, ...), kind=kLoop, calls=%fused_computation.68 | loop fusion | flops 29884416 | bytes 6291532 | tf_op jit(solution)/shard_map/mul | solution.py:40
  38.2 13.3 %fusion.27 = f32[1,512,4,128]{1,3,2,0:T(8,128)S(1)} fusion(f32[512,1,4,128]{0,3,2,1:T(8,128)S(1)} %get-tuple-element.6, f32[]{:T(128)} %bitcast.87, f32[]{:T(128)} %bitcast.85, f32[]{:T(128)} %bitcast.83, f32[]{:T(128)} %bitcast.81, f32[]{:T(128)} %bitcast.79, f32[]{:T(128)} %bitcast.77, f32[]{:T(128)} %bitcast.75, f32[]{:T(128)} %bitcast.73, f32[]{:T(128)} %bitcast.71, ...), kind=kLoop, calls=%fused_computation.60 | loop fusion | flops 25952256 | bytes 3145792 | tf_op jit(solution)/shard_map/mul | solution.py:40
  51.5 13.4 %fusion.26 = f32[1,512,4,128]{1,3,2,0:T(8,128)S(1)} fusion(f32[512,1,4,128]{0,3,2,1:T(8,128)S(1)} %get-tuple-element.6, f32[]{:T(128)} %bitcast.112, f32[]{:T(128)} %bitcast.110, f32[]{:T(128)} %bitcast.108, f32[]{:T(128)} %bitcast.106, f32[]{:T(128)} %bitcast.104, f32[]{:T(128)} %bitcast.102, f32[]{:T(128)} %bitcast.100, f32[]{:T(128)} %bitcast.98, ...), kind=kLoop, calls=%fused_computation.51 | loop fusion | flops 25952256 | bytes 3145792 | tf_op jit(solution)/shard_map/mul | solution.py:40
  64.9 13.6 %bitcast_add_fusion.24 = f32[1,512,4,128]{1,3,2,0:T(8,128)S(1)} fusion(f32[]{:T(128)} %bitcast.33, f32[]{:T(128)} %bitcast.31, f32[]{:T(128)} %bitcast.29, f32[]{:T(128)} %bitcast.27, f32[]{:T(128)} %bitcast.25, f32[]{:T(128)} %bitcast.23, f32[]{:T(128)} %bitcast.21, f32[]{:T(128)} %bitcast.19, f32[]{:T(128)} %bitcast.17, f32[]{:T(128)} %bitcast.16, ...), kind=kLoop, calls=%fused_computation.77 | loop fusion | flops 25690112 | bytes 2097216 | tf_op jit(solution)/shard_map/add | solution.py:34
  79.6 1.3 %select_maximum_fusion = f32[4,512,8,128]{1,3,2,0:T(8,128)S(1)} fusion(f32[4,512,4,32]{1,3,2,0:T(8,128)S(1)} %get-tuple-element.8, f32[4,512,4,32]{1,3,2,0:T(8,128)S(1)} %get-tuple-element.9, f32[4,512,4,32]{1,3,2,0:T(8,128)S(1)} %get-tuple-element.10, f32[4,512,4,32]{1,3,2,0:T(8,128)S(1)} %get-tuple-element.7), kind=kLoop, calls=%fused_computation.4 | loop fusion | flops 31457280 | bytes 12582912 | tf_op jit(solution)/shard_map/concatenate | solution.py:89
  80.9 2.4 %subtract_multiply_fusion = f32[512,8,128]{0,2,1:T(8,128)S(1)} fusion(f32[4,512,8,128]{1,3,2,0:T(8,128)S(1)} %select_maximum_fusion, s32[512,8]{0,1:T(8,128)S(1)} %get-tuple-element.26, s32[512,8]{0,1:T(8,128)S(1)} %get-tuple-element.25, s32[128]{0:T(128)S(1)} %iota_add_fusion), kind=kOutput, calls=%fused_computation.25 | convolution fusion | flops 812662784 | bytes 6358016 | tf_op jit(solution)/shard_map/dot_general | solution.py:105
  83.8 1.1 %fusion.2 = f32[3,512,8]{1,2,0:T(8,128)S(1)} fusion(f32[4,512,8,128]{1,3,2,0:T(8,128)S(1)} %select_maximum_fusion, f32[512,8,128]{0,2,1:T(8,128)S(1)} %subtract_multiply_fusion), kind=kLoop, calls=%fused_computation.12 | loop fusion | flops 3133440 | bytes 8437760 | tf_op jit(solution)/shard_map/reduce_sum | solution.py:109
  85.0 1.9 %collective-permute-start.4 = (f32[4,4,512]{2,1,0:T(4,128)S(1)}, f32[4,4,512]{2,1,0:T(4,128)S(1)}, u32[]{:S(2)}, u32[]{:S(2)}) collective-permute-start(f32[4,4,512]{2,1,0:T(4,128)S(1)} %slice.433), channel_id=1, source_target_pairs={{0,2},{2,4},{4,6},{6,8},{8,10},{10,12},{12,14},{14,16},{16,18},{18... | collective-permute-start | bytes 98312 | tf_op jit(solution)/shard_map/ppermute | solution.py:23
  86.9 4.2 %collective-permute-done.4 = f32[4,4,512]{2,1,0:T(4,128)S(1)} collective-permute-done((f32[4,4,512]{2,1,0:T(4,128)S(1)}, f32[4,4,512]{2,1,0:T(4,128)S(1)}, u32[]{:S(2)}, u32[]{:S(2)}) %collective-permute-start.4) | collective-permute-done | bytes 32800 | tf_op jit(solution)/shard_map/ppermute | solution.py:23
  91.2 1.9 %collective-permute-start.5 = (f32[4,4,512]{2,1,0:T(4,128)S(1)}, f32[4,4,512]{2,1,0:T(4,128)S(1)}, u32[]{:S(2)}, u32[]{:S(2)}) collective-permute-start(f32[4,4,512]{2,1,0:T(4,128)S(1)} %pad_maximum_fusion.9), channel_id=1, source_target_pairs={{0,2},{2,4},{4,6},{6,8},{8,10},{10,12},{12,14},{14,16},{16,18},{18... | collective-permute-start | bytes 98312 | tf_op jit(solution)/shard_map/ppermute | solution.py:23
  93.2 4.2 %collective-permute-done.5 = f32[4,4,512]{2,1,0:T(4,128)S(1)} collective-permute-done((f32[4,4,512]{2,1,0:T(4,128)S(1)}, f32[4,4,512]{2,1,0:T(4,128)S(1)}, u32[]{:S(2)}, u32[]{:S(2)}) %collective-permute-start.5) | collective-permute-done | bytes 32800 | tf_op jit(solution)/shard_map/ppermute | solution.py:23
  97.4 4.8 %all-gather = f32[8,4,512]{2,1,0:T(4,128)S(1)} all-gather(f32[4,4,512]{2,1,0:T(4,128)S(1)} %select_select_fusion), channel_id=2, replica_groups=mesh['plane'=16,'depth'=2] {'depth'}, dimensions={0}, use_global_device_ids=true | all-gather | bytes 98304 | tf_op jit(solution)/shard_map/all_gather | solution.py:124
  (32 shorter events, 4.4 us)
Async XLA Ops:
  0.0 21.2 %copy-start = (bf16[512,512]{1,0:T(8,128)(2,1)S(1)}, bf16[512,512]{1,0:T(8,128)(2,1)}, u32[]{:S(2)}) copy-start(bf16[512,512]{1,0:T(8,128)(2,1)} %param.6) | copy-start | bytes 1572868
  0.0 6.4 %copy-start.1 = (f32[16,4]{0,1:T(4,128)S(1)}, f32[16,4]{0,1:T(4,128)}, u32[]{:S(2)}) copy-start(f32[16,4]{0,1:T(4,128)} %param.7) | copy-start | bytes 772
  0.0 10.1 %copy-start.3 = (f32[3]{0:T(128)S(1)}, f32[3]{0:T(128)}, u32[]{:S(2)}) copy-start(f32[3]{0:T(128)} %param.8) | copy-start | bytes 40
  1.7 9.1 %collective-permute-start = (f32[1,512,128]{1,2,0:T(8,128)S(1)}, f32[1,512,128]{1,2,0:T(8,128)S(1)}, u32[]{:S(2)}, u32[]{:S(2)}) collective-permute-start(f32[1,512,128]{1,2,0:T(8,128)S(1)} %get-tuple-element.18), channel_id=1, source_target_pairs={{2,0},{4,2},{6,4},{8,6},{10,8},{12,10},{14,12},{16,14},{18,16},{20... | collective-permute-start | bytes 786440 | tf_op jit(solution)/shard_map/ppermute | solution.py:15
  4.4 8.6 %collective-permute-start.1 = (f32[1,512,128]{1,2,0:T(8,128)S(1)}, f32[1,512,128]{1,2,0:T(8,128)S(1)}, u32[]{:S(2)}, u32[]{:S(2)}) collective-permute-start(f32[1,512,128]{1,2,0:T(8,128)S(1)} %get-tuple-element.17), channel_id=1, source_target_pairs={{0,2},{2,4},{4,6},{6,8},{8,10},{10,12},{12,14},{14,16},{16,18},{18... | collective-permute-start | bytes 786440 | tf_op jit(solution)/shard_map/ppermute | solution.py:12
  13.1 5.9 %collective-permute-start.2 = (f32[6,512,1]{1,2,0:T(1,128)S(1)}, f32[6,512,1]{1,2,0:T(1,128)S(1)}, u32[]{:S(2)}, u32[]{:S(2)}) collective-permute-start(f32[6,512,1]{1,2,0:T(1,128)S(1)} %get-tuple-element.13), channel_id=1, source_target_pairs={{1,0},{3,2},{5,4},{7,6},{9,8},{11,10},{13,12},{15,14},{17,16},{19,... | collective-permute-start | bytes 36872 | tf_op jit(solution)/shard_map/ppermute | solution.py:15
  14.3 5.9 %collective-permute-start.3 = (f32[6,512,1]{1,2,0:T(1,128)S(1)}, f32[6,512,1]{1,2,0:T(1,128)S(1)}, u32[]{:S(2)}, u32[]{:S(2)}) collective-permute-start(f32[6,512,1]{1,2,0:T(1,128)S(1)} %get-tuple-element.14), channel_id=1, source_target_pairs={{0,1},{2,3},{4,5},{6,7},{8,9},{10,11},{12,13},{14,15},{16,17},{18,... | collective-permute-start | bytes 36872 | tf_op jit(solution)/shard_map/ppermute | solution.py:12
  83.8 7.3 %copy-start.2 = (f32[4,4,512]{2,1,0:T(4,128)S(1)}, f32[4,4,512]{2,1,0:T(4,128)}, u32[]{:S(2)}) copy-start(f32[4,4,512]{2,1,0:T(4,128)} %constant.38.clone.1) | copy-start | bytes 98308
  85.0 6.1 %collective-permute-start.4 = (f32[4,4,512]{2,1,0:T(4,128)S(1)}, f32[4,4,512]{2,1,0:T(4,128)S(1)}, u32[]{:S(2)}, u32[]{:S(2)}) collective-permute-start(f32[4,4,512]{2,1,0:T(4,128)S(1)} %slice.433), channel_id=1, source_target_pairs={{0,2},{2,4},{4,6},{6,8},{8,10},{10,12},{12,14},{14,16},{16,18},{18... | collective-permute-start | bytes 98312 | tf_op jit(solution)/shard_map/ppermute | solution.py:23
  91.2 6.1 %collective-permute-start.5 = (f32[4,4,512]{2,1,0:T(4,128)S(1)}, f32[4,4,512]{2,1,0:T(4,128)S(1)}, u32[]{:S(2)}, u32[]{:S(2)}) collective-permute-start(f32[4,4,512]{2,1,0:T(4,128)S(1)} %pad_maximum_fusion.9), channel_id=1, source_target_pairs={{0,2},{2,4},{4,6},{6,8},{8,10},{10,12},{12,14},{14,16},{16,18},{18... | collective-permute-start | bytes 98312 | tf_op jit(solution)/shard_map/ppermute | solution.py:23
where the time goes:
time: 104 us; the launch traced here: 103 us
  other arithmetic  61.1 us (59%)
  starting transfers between devices  14.3 us (14%)
  waiting for transfers between devices  12 us (12%)
  local copies, waits for them, and re-layouts  6.49 us (6%)
  blocking collectives  4.84 us (5%)
  matrix products  3.67 us (4%)
    mul x3, other arithmetic, shade(): return (sigma, red * lit, green * lit, blue * lit)  42.4 us
    add x1, other arithmetic, shade(): sigma = sigma + hat * transfer[knot, 3]  13.6 us
    ppermute x2, waiting for transfers between devices, passed_along(): lax.ppermute(value, axis, [(source, source + steps) for source in range(f...  8.39 us
    ppermute x2, starting transfers between devices, extended(): lax.ppermute(lax.slice_in_dim(block, block.shape[dim] - width, None, axis...  6.46 us
    all_gather x1, blocking collectives, body(): gathered = lax.all_gather(aligned[None], 'depth', axis=0, tiled=True)  4.84 us
    ppermute x2, starting transfers between devices, extended(): lax.ppermute(lax.slice_in_dim(block, 0, width, axis=dim), axis, backward)  4.05 us
    ppermute x2, starting transfers between devices, passed_along(): lax.ppermute(value, axis, [(source, source + steps) for source in range(f...  3.84 us
    ppermute x2, waiting for transfers between devices, extended(): lax.ppermute(lax.slice_in_dim(block, block.shape[dim] - width, None, axis...  3.65 us
  transfers between devices with their start and end apart: 6, of which 4 were waited for; matrix products, arithmetic and copies ran while one was open for 4% of the time, Pallas kernels for 0%

commit v1 on v0

v1 whole, which is shorter than its diff:
```python
import functools

import jax
import jax.numpy as jnp
from jax import lax
from jax.experimental import pallas as pl
from jax.experimental.pallas import tpu as pltpu
from jax.sharding import PartitionSpec as P

MESH = pl.DeviceIdType.MESH
PAD = 8


def kernel(
    planes, depths, volume, resample, bounds, transfer, light, out,
    vol, mat, rows, window, side_x, edge, side_z, tall, fields, samples, taus, before, tint, pieces,
    table, send, recv, local_sem, x_send, x_recv, z_send, z_recv, p_send, p_recv,
):
    cells_x, cells_y, cells_z = volume.shape
    knots = transfer.shape[0]
    columns = bounds.shape[1]
    share = cells_y // depths
    group = cells_z // cells_x
    lanes = 128
    p = lax.axis_index("plane")
    d = lax.axis_index("depth")

    loads = [pltpu.make_async_copy(volume.at[x], vol.at[x], local_sem.at[x]) for x in range(cells_x)]
    loads.append(pltpu.make_async_copy(resample, mat, local_sem.at[cells_x]))
    loads.append(pltpu.make_async_copy(bounds, rows.at[:, :columns], local_sem.at[cells_x + 1]))
    for load in loads:
        load.start()

    barrier = pltpu.get_barrier_semaphore()

    def greet(condition, plane, depth):
        @pl.when(condition)
        def _():
            pl.semaphore_signal(barrier, inc=1, device_id=(plane, depth), device_id_type=MESH)

    greet(p > 0, p - 1, d)
    greet(p < planes - 1, p + 1, d)
    greet(d > 0, p, d - 1)
    greet(d < depths - 1, p, d + 1)
    for source in range(depths):
        low_there = p - source >= 0
        if source == 0:
            low_there = low_there & (d != 0)
        greet(low_there, p - source, source)
        greet(p - source - 1 >= 0, p - source - 1, source)

    table[...] = jnp.zeros_like(table)
    table[:knots, : transfer.shape[1]] = transfer[...]
    flat = table[...].T[:8]
    knot_index = lax.broadcasted_iota(jnp.int32, flat.shape, 1)
    slope = jnp.where(knot_index < knots - 1, pltpu.roll(flat, lanes - 1, 1) - flat, 0.0)
    table[:8] = flat
    table[8:16] = slope

    for x in range(cells_x):
        loads[x].wait()

    def turn(x, carry):
        turned = vol[x].T
        tall[x + 1, PAD : PAD + cells_z] = turned
        fields[0, x] = turned.astype(jnp.bfloat16)
        edge[0, x] = turned[:1]
        edge[1, x] = turned[cells_z - 1 :]
        return carry

    lax.fori_loop(0, cells_x, turn, 0)

    def one(condition):
        return jnp.where(condition, 1, 0)

    partners = one(p > 0) + one(p < planes - 1) + one(d > 0) + one(d < depths - 1)
    partners += one(p + d < planes) * (depths - one(d == 0))
    partners += one(p + d + 1 < planes) * depths
    pl.semaphore_wait(barrier, partners)

    def remote(src, dst, send_sem, recv_sem, plane, depth):
        return pltpu.make_async_remote_copy(
            src_ref=src, dst_ref=dst, send_sem=send_sem, recv_sem=recv_sem,
            device_id=(plane, depth), device_id_type=MESH,
        )

    x_up = remote(vol.at[cells_x - 1], side_x.at[0], x_send.at[0], x_recv.at[0], p + 1, d)
    x_down = remote(vol.at[0], side_x.at[1], x_send.at[1], x_recv.at[1], p - 1, d)
    z_up = remote(edge.at[1], side_z.at[0], z_send.at[0], z_recv.at[0], p, d + 1)
    z_down = remote(edge.at[0], side_z.at[1], z_send.at[1], z_recv.at[1], p, d - 1)
    has_below, has_above = p > 0, p < planes - 1
    has_front, has_back = d > 0, d < depths - 1
    pl.when(has_above)(x_up.start)
    pl.when(has_below)(x_down.start)
    pl.when(has_back)(z_up.start)
    pl.when(has_front)(z_down.start)

    def resampled(field, first, count):
        for x in range(first, first + count):
            samples[field, x] = lax.dot_general(
                fields[field, x], mat[...], (((1,), (1,)), ((), ())),
                preferred_element_type=jnp.float32,
            )

    loads[cells_x].wait()
    resampled(0, 0, cells_x)

    def slope_y(step, carry):
        x, part = step // cells_x, step % cells_x
        block = tall[x + 1, pl.ds(pl.multiple_of(PAD + part * group, 8), group)]
        lane = lax.broadcasted_iota(jnp.int32, block.shape, 1)
        upper = jnp.where(lane < cells_y - 1, pltpu.roll(block, cells_y - 1, 1), 0.0)
        lower = jnp.where(lane > 0, pltpu.roll(block, 1, 1), 0.0)
        fields[2, x, pl.ds(pl.multiple_of(part * group, 16), group)] = (
            (upper - lower) * 0.5
        ).astype(jnp.bfloat16)
        return carry

    lax.fori_loop(0, cells_x * cells_x, slope_y, 0)
    resampled(2, 0, cells_x)

    loads[cells_x + 1].wait()
    rows[:, columns:] = jnp.zeros_like(rows[:, columns:])
    nearest = jnp.minimum(p + d, planes - 1) * cells_x
    offset = nearest % 8
    around = pl.ds(pl.multiple_of(nearest - offset, 8), 16)
    for end in range(2):
        found = rows[end, around]
        aligned = jnp.where(offset == 0, found[: 2 * cells_x], found[8 - cells_x : 8 + cells_x])
        for pixel in range(2 * cells_x):
            window[end, pixel] = aligned[pixel : pixel + 1]

    scale = (knots - 1) / 5.0
    step_size = 2.0 / (depths * cells_z)

    def density(step, carry):
        x, part = step // cells_x, step % cells_x
        at = pl.ds(pl.multiple_of(part * group, 16), group)
        index = d * cells_z + part * group + lax.broadcasted_iota(jnp.int32, (group, lanes), 0)
        for tile in range(cells_y // lanes):
            here = slice(tile * lanes, (tile + 1) * lanes)
            spot = jnp.clip(samples[0, x, at, here] * scale + 2.5 * scale, 0.0, knots - 1.0)
            knot = spot.astype(jnp.int32)
            rest = spot - knot.astype(jnp.float32)

            def looked_up(channel):
                base = jnp.broadcast_to(table[channel : channel + 1], (group, lanes))
                tilt = jnp.broadcast_to(table[8 + channel : 9 + channel], (group, lanes))
                return jnp.take_along_axis(
                    base, knot, axis=1, mode="promise_in_bounds"
                ) + rest * jnp.take_along_axis(tilt, knot, axis=1, mode="promise_in_bounds")

            first = window[0, x + part, :, here]
            last = window[1, x + part, :, here]
            inside = (index >= first) & (index < last)
            taus[x, at, here] = jnp.where(inside, step_size * looked_up(3), 0.0)
            for channel in range(3):
                tint[channel, x, at, here] = looked_up(channel)
        return carry

    lax.fori_loop(0, cells_x * cells_x, density, 0)

    row = lax.broadcasted_iota(jnp.int32, (cells_z, cells_z), 0)
    column = lax.broadcasted_iota(jnp.int32, (cells_z, cells_z), 1)
    earlier = jnp.where((column < row) & (column // group == row // group), 1.0, 0.0)
    earlier = earlier.astype(jnp.bfloat16)
    for x in range(cells_x):
        tau = taus[x]
        high = tau.astype(jnp.bfloat16)
        low = (tau - high.astype(jnp.float32)).astype(jnp.bfloat16)
        before[x] = jnp.dot(earlier, high, preferred_element_type=jnp.float32) + jnp.dot(
            earlier, low, preferred_element_type=jnp.float32
        )

    pl.when(has_front)(z_down.wait_send)
    pl.when(has_back)(z_up.wait_send)
    pl.when(has_front)(z_up.wait_recv)
    pl.when(has_back)(z_down.wait_recv)

    @pl.when(jnp.logical_not(has_front))
    def _():
        side_z[0] = jnp.zeros_like(side_z[0])

    @pl.when(jnp.logical_not(has_back))
    def _():
        side_z[1] = jnp.zeros_like(side_z[1])

    for x in range(cells_x):
        tall[x + 1, PAD - 1 : PAD] = side_z[0, x]
        tall[x + 1, PAD + cells_z : PAD + cells_z + 1] = side_z[1, x]
    for x in range(cells_x):
        ahead = tall[x + 1, PAD + 1 : PAD + 1 + cells_z]
        behind = tall[x + 1, PAD - 1 : PAD - 1 + cells_z]
        fields[3, x] = ((ahead - behind) * 0.5).astype(jnp.bfloat16)
    resampled(3, 0, cells_x)

    def slope_x(x, carry):
        ahead = tall[x + 2, PAD : PAD + cells_z]
        behind = tall[x, PAD : PAD + cells_z]
        fields[1, x] = ((ahead - behind) * 0.5).astype(jnp.bfloat16)
        return carry

    lax.fori_loop(1, cells_x - 1, slope_x, 0)
    resampled(1, 1, cells_x - 2)
    pl.when(has_above)(x_up.wait_send)
    pl.when(has_below)(x_down.wait_send)
    pl.when(has_below)(x_up.wait_recv)
    pl.when(has_above)(x_down.wait_recv)

    @pl.when(jnp.logical_not(has_below))
    def _():
        side_x[0] = jnp.zeros_like(side_x[0])

    @pl.when(jnp.logical_not(has_above))
    def _():
        side_x[1] = jnp.zeros_like(side_x[1])

    tall[0, PAD : PAD + cells_z] = side_x[0].T
    tall[cells_x + 1, PAD : PAD + cells_z] = side_x[1].T
    slope_x(0, 0)
    slope_x(cells_x - 1, 0)
    resampled(1, 0, 1)
    resampled(1, cells_x - 1, 1)

    light_x, light_y, light_z = light[0], light[1], light[2]

    def composite(step, carry):
        x, part = step // cells_x, step % cells_x
        at = pl.ds(pl.multiple_of(part * group, 16), group)
        for tile in range(cells_y // lanes):
            here = slice(tile * lanes, (tile + 1) * lanes)
            grad_x = samples[1, x, at, here]
            grad_y = samples[2, x, at, here]
            grad_z = samples[3, x, at, here]
            lit = jnp.abs(grad_x * light_x + grad_y * light_y + grad_z * light_z)
            norm = grad_x * grad_x + grad_y * grad_y + grad_z * grad_z + 1.0
            lit = 0.3 + 0.7 * lit * lax.rsqrt(norm)
            tau = taus[x, at, here]
            weight = jnp.exp(-before[x, at, here]) * (1.0 - jnp.exp(-tau)) * lit
            for channel in range(3):
                pieces[part, channel, x, :, here] = jnp.sum(
                    weight * tint[channel, x, at, here], axis=0, keepdims=True
                )
            pieces[part, 3, x, :, here] = jnp.sum(tau, axis=0, keepdims=True)
        return carry

    lax.fori_loop(0, cells_x * cells_x, composite, 0)

    def placed(part, channel):
        ahead = [jnp.zeros((part, cells_y), jnp.float32)] if part else []
        block = [pieces[part, channel, x] for x in range(cells_x)]
        rest = [jnp.zeros((cells_x - part, cells_y), jnp.float32)]
        return jnp.concatenate(ahead + block + rest, axis=0)

    color, remain = None, None
    for part in range(cells_x - 1, -1, -1):
        clear = jnp.exp(-placed(part, 3))
        front = [placed(part, channel) for channel in range(3)]
        if color is None:
            color, remain = front, clear
        else:
            color = [front[channel] + clear * color[channel] for channel in range(3)]
            remain = clear * remain
    for channel, value in enumerate(color + [remain]):
        for half in range(2):
            for block in range(depths):
                send[half, block, channel] = value[
                    half * cells_x : (half + 1) * cells_x, block * share : (block + 1) * share
                ]

    sends = []
    for half in range(2):
        for block in range(depths):
            there = p + d + half < planes
            if half == 0 and block == 0:
                there = there & (d != 0)
            copy = remote(
                send.at[half, block], recv.at[d, half], p_send.at[half, block],
                p_recv.at[d, half], p + d + half, block,
            )
            pl.when(there)(copy.start)
            sends.append((there, copy))

    @pl.when(d == 0)
    def _():
        recv[0, 0] = send[0, 0]

    for source in range(depths):
        for half in range(2):
            there = p - source - half >= 0

            @pl.when(jnp.logical_not(there))
            def _():
                recv[source, half, :3] = jnp.zeros_like(recv[source, half, :3])
                recv[source, half, 3] = jnp.ones_like(recv[source, half, 3])

            if half == 0 and source == 0:
                there = there & (d != 0)
            arrival = remote(
                send.at[half, 0], recv.at[source, half], p_send.at[half, 0],
                p_recv.at[source, half], p, d,
            )
            pl.when(there)(arrival.wait_recv)

    color = [recv[0, 0, channel] for channel in range(3)]
    remain = recv[0, 0, 3]
    for source in range(depths):
        for half in range(2):
            if source == 0 and half == 0:
                continue
            color = [
                color[channel] + remain * recv[source, half, channel] for channel in range(3)
            ]
            remain = remain * recv[source, half, 3]
    for channel in range(3):
        out[channel] = color[channel]
    out[3] = 1.0 - remain
    for there, copy in sends:
        pl.when(there)(copy.wait_send)


def body(volume, resample, transfer, light, ray_bounds):
    cells_x, cells_y, cells_z = volume.shape
    planes = lax.axis_size("plane")
    depths = lax.axis_size("depth")
    share = cells_y // depths
    f32 = jnp.float32
    dma = pltpu.SemaphoreType.DMA
    return pl.pallas_call(
        functools.partial(kernel, planes, depths),
        out_shape=jax.ShapeDtypeStruct((4, cells_x, share), f32),
        in_specs=[
            pl.BlockSpec(memory_space=pl.ANY),
            pl.BlockSpec(memory_space=pl.ANY),
            pl.BlockSpec(memory_space=pl.ANY),
            pl.BlockSpec(memory_space=pltpu.VMEM),
            pl.BlockSpec(memory_space=pltpu.SMEM),
        ],
        out_specs=pl.BlockSpec(memory_space=pltpu.VMEM),
        scratch_shapes=[
            pltpu.VMEM((cells_x, cells_y, cells_z), f32),
            pltpu.VMEM(resample.shape, resample.dtype),
            pltpu.VMEM((2, ray_bounds.shape[1] + 8, cells_y), ray_bounds.dtype),
            pltpu.VMEM((2, 2 * cells_x, 1, cells_y), ray_bounds.dtype),
            pltpu.VMEM((2, cells_y, cells_z), f32),
            pltpu.VMEM((2, cells_x, 1, cells_y), f32),
            pltpu.VMEM((2, cells_x, 1, cells_y), f32),
            pltpu.VMEM((cells_x + 2, cells_z + 2 * PAD, cells_y), f32),
            pltpu.VMEM((4, cells_x, cells_z, cells_y), jnp.bfloat16),
            pltpu.VMEM((4, cells_x, cells_z, cells_y), f32),
            pltpu.VMEM((cells_x, cells_z, cells_y), f32),
            pltpu.VMEM((cells_x, cells_z, cells_y), f32),
            pltpu.VMEM((3, cells_x, cells_z, cells_y), f32),
            pltpu.VMEM((cells_x, 4, cells_x, 1, cells_y), f32),
            pltpu.VMEM((128, 128), f32),
            pltpu.VMEM((2, depths, 4, cells_x, share), f32),
            pltpu.VMEM((depths, 2, 4, cells_x, share), f32),
            dma((cells_x + 2,)),
            dma((2,)),
            dma((2,)),
            dma((2,)),
            dma((2,)),
            dma((2, depths)),
            dma((depths, 2)),
        ],
        compiler_params=pltpu.CompilerParams(
            collective_id=0, has_side_effects=True, vmem_limit_bytes=40 * 1024 * 1024
        ),
    )(volume, resample, ray_bounds, transfer, light)


def solution(mesh):
    in_specs = (P("plane", None, "depth"), P(), P(), P(), P())
    out_specs = P(None, "plane", "depth")
    return jax.shard_map(body, mesh=mesh, in_specs=in_specs, out_specs=out_specs, check_vma=False)
```

time: 104 us -> 25.8 us (0.25)
  other arithmetic: 61.1 us -> 0 us
  Pallas kernels: 0 us -> 21 us
  starting transfers between devices: 14.3 us -> 0 us
  waiting for transfers between devices: 12 us -> 0 us
  blocking collectives: 4.84 us -> 0 us
  matrix products: 3.67 us -> 0 us
  local copies, waits for them, and re-layouts: 6.49 us -> 4.6 us
    mul x4 -> x0, other arithmetic: 42.4 us -> none  [the longest x3 42.4 us: shade(): return (sigma, red * lit, green * lit, blue * lit)]
    pallas_call x0 -> x1, Pallas kernels: none -> 21 us  [body(): pl.pallas_call(functools.partial(kernel, planes, depths), out_shape=jax.S...]
    ppermute x6 -> x0, starting transfers between devices: 14.3 us -> none  [the longest x2 6.46 us: extended(): lax.ppermute(lax.slice_in_dim(block, block.shape[dim] - width, None, axis...]
    add x4 -> x0, other arithmetic: 13.6 us -> none  [the longest x1 13.6 us: shade(): sigma = sigma + hat * transfer[knot, 3]]
    ppermute x6 -> x0, waiting for transfers between devices: 12 us -> none  [the longest x2 8.39 us: passed_along(): lax.ppermute(value, axis, [(source, source + steps) for source in range(f...]
    all_gather x1 -> x0, blocking collectives: 4.84 us -> none  [body(): gathered = lax.all_gather(aligned[None], 'depth', axis=0, tiled=True)]
    slice x8 -> x0, local copies, waits for them, and re-layouts: 4.02 us -> none  [the longest x4 2.86 us: shade(): sigma = sigma + hat * transfer[knot, 3]]
    dot_general x2 -> x0, matrix products: 3.67 us -> none  [the longest x1 2.38 us: body(): jnp.dot(tau.reshape(-1, cells_z), earlier, precision=lax.Precision.HIGHEST)]
  transfers between devices with their start and end apart: 6 -> 0, of which waited for: 4 -> 0; matrix products, arithmetic and copies ran while one was open for 4% -> 0% of each run, Pallas kernels for 0% -> 0%
where the time goes in v1:
time: 25.8 us; the launch traced here: 25.6 us
  Pallas kernels  21 us (81%)
  local copies, waits for them, and re-layouts  4.6 us (18%)
    pallas_call x1, Pallas kernels, body(): pl.pallas_call(functools.partial(kernel, planes, depths), out_shape=jax.S...  21 us
    unnamed x10, local copies, waits for them, and re-layouts  4.6 us

profile of v1, /device:TPU:16, one launch (start us, length us, event | category | flops | bytes accessed | tf_op | source)
XLA Modules:
  0.0 25.6 jit_solution(13547821864655594972)
XLA Ops:
  0.0 0.0 copy-start.3
  0.0 0.8 %copy.6.transfer = f32[16,4]{1,0:T(8,128)S(1)} copy(f32[16,4]{0,1:T(4,128)} %param.7) | data formatting | bytes 512 | tf_op args[2]
  0.8 0.0 copy-done.3
  0.8 0.0 copy-start
  0.8 1.2 %copy-done = f32[4,512,128]{2,1,0:T(8,128)S(1)} copy-done((f32[4,512,128]{2,1,0:T(8,128)S(1)}, f32[4,512,128]{2,1,0:T(8,128)}, u32[]{:S(2)}) %copy-start) | copy-done | bytes 1048600
  2.0 0.0 copy-start.1
  2.0 1.0 %copy-done.1 = bf16[512,512]{1,0:T(8,128)(2,1)S(1)} copy-done((bf16[512,512]{1,0:T(8,128)(2,1)S(1)}, bf16[512,512]{1,0:T(8,128)(2,1)}, u32[]{:S(2)}) %copy-start.1) | copy-done | bytes 524312
  3.0 0.0 copy-start.2
  3.0 0.9 %copy-done.2 = s32[2,64,512]{2,1,0:T(8,128)S(1)} copy-done((s32[2,64,512]{2,1,0:T(8,128)S(1)}, s32[2,64,512]{2,1,0:T(8,128)}, u32[]{:S(2)}) %copy-start.2) | copy-done | bytes 262168
  4.0 21.0 %shard_map.55 = f32[4,4,256]{2,1,0:T(4,128)S(1)} custom-call(f32[4,512,128]{2,1,0:T(8,128)S(1)} %copy-done, bf16[512,512]{1,0:T(8,128)(2,1)S(1)} %copy-done.1, s32[2,64,512]{2,1,0:T(8,128)S(1)} %copy-done.2, f32[16,4]{1,0:T(8,128)S(1)} %copy.6.transfer, f32[3]{0:T(128)S(1)} %copy-done.3), custom_call_target="tpu_custom_call" | custom-call | tf_op jit(solution)/shard_map/pallas_call | solution.py:329
  25.0 0.6 %copy.8 = f32[4,4,256]{2,1,0:T(4,128)} copy(f32[4,4,256]{2,1,0:T(4,128)S(1)} %shard_map.55) | data formatting | bytes 32768
Async XLA Ops:
  0.0 0.8 %copy-start.3 = (f32[3]{0:T(128)S(1)}, f32[3]{0:T(128)}, u32[]{:S(2)}) copy-start(f32[3]{0:T(128)} %light.1) | copy-start | bytes 40
  0.8 1.2 %copy-start = (f32[4,512,128]{2,1,0:T(8,128)S(1)}, f32[4,512,128]{2,1,0:T(8,128)}, u32[]{:S(2)}) copy-start(f32[4,512,128]{2,1,0:T(8,128)} %volume.1) | copy-start | bytes 3145732
  2.0 1.0 %copy-start.1 = (bf16[512,512]{1,0:T(8,128)(2,1)S(1)}, bf16[512,512]{1,0:T(8,128)(2,1)}, u32[]{:S(2)}) copy-start(bf16[512,512]{1,0:T(8,128)(2,1)} %resample.1) | copy-start | bytes 1572868
  3.0 0.9 %copy-start.2 = (s32[2,64,512]{2,1,0:T(8,128)S(1)}, s32[2,64,512]{2,1,0:T(8,128)}, u32[]{:S(2)}) copy-start(s32[2,64,512]{2,1,0:T(8,128)} %bounds.1) | copy-start | bytes 786436

commit v2 on v1

--- a/solution.py
+++ b/solution.py
@@ -17,7 +17,7 @@
     table, send, recv, local_sem, x_send, x_recv, z_send, z_recv, p_send, p_recv,
 ):
     cells_x, cells_y, cells_z = volume.shape
-    knots = transfer.shape[0]
+    channels, knots = transfer.shape
     columns = bounds.shape[1]
     share = cells_y // depths
     group = cells_z // cells_x
@@ -50,13 +50,34 @@
         greet(p - source - 1 >= 0, p - source - 1, source)
 
     table[...] = jnp.zeros_like(table)
-    table[:knots, : transfer.shape[1]] = transfer[...]
-    flat = table[...].T[:8]
+    table[:channels, :knots] = transfer[...]
+    flat = table[:8]
     knot_index = lax.broadcasted_iota(jnp.int32, flat.shape, 1)
     slope = jnp.where(knot_index < knots - 1, pltpu.roll(flat, lanes - 1, 1) - flat, 0.0)
-    table[:8] = flat
     table[8:16] = slope
 
+    def one(condition):
+        return jnp.where(condition, 1, 0)
+
+    partners = one(p > 0) + one(p < planes - 1) + one(d > 0) + one(d < depths - 1)
+    partners += one(p + d < planes) * (depths - one(d == 0))
+    partners += one(p + d + 1 < planes) * depths
+    pl.semaphore_wait(barrier, partners)
+
+    def remote(src, dst, send_sem, recv_sem, plane, depth):
+        return pltpu.make_async_remote_copy(
+            src_ref=src, dst_ref=dst, send_sem=send_sem, recv_sem=recv_sem,
+            device_id=(plane, depth), device_id_type=MESH,
+        )
+
+    x_up = remote(volume.at[cells_x - 1], side_x.at[0], x_send.at[0], x_recv.at[0], p + 1, d)
+    x_down = remote(volume.at[0], side_x.at[1], x_send.at[1], x_recv.at[1], p - 1, d)
+    z_up = remote(edge.at[1], side_z.at[0], z_send.at[0], z_recv.at[0], p, d + 1)
+    z_down = remote(edge.at[0], side_z.at[1], z_send.at[1], z_recv.at[1], p, d - 1)
+    has_below, has_above = p > 0, p < planes - 1
+    has_front, has_back = d > 0, d < depths - 1
+    pl.when(has_above)(x_up.start)
+    pl.when(has_below)(x_down.start)
     for x in range(cells_x):
         loads[x].wait()
 
@@ -68,39 +89,17 @@
         edge[1, x] = turned[cells_z - 1 :]
         return carry
 
-    lax.fori_loop(0, cells_x, turn, 0)
-
-    def one(condition):
-        return jnp.where(condition, 1, 0)
-
-    partners = one(p > 0) + one(p < planes - 1) + one(d > 0) + one(d < depths - 1)
-    partners += one(p + d < planes) * (depths - one(d == 0))
-    partners += one(p + d + 1 < planes) * depths
-    pl.semaphore_wait(barrier, partners)
-
-    def remote(src, dst, send_sem, recv_sem, plane, depth):
-        return pltpu.make_async_remote_copy(
-            src_ref=src, dst_ref=dst, send_sem=send_sem, recv_sem=recv_sem,
-            device_id=(plane, depth), device_id_type=MESH,
-        )
-
-    x_up = remote(vol.at[cells_x - 1], side_x.at[0], x_send.at[0], x_recv.at[0], p + 1, d)
-    x_down = remote(vol.at[0], side_x.at[1], x_send.at[1], x_recv.at[1], p - 1, d)
-    z_up = remote(edge.at[1], side_z.at[0], z_send.at[0], z_recv.at[0], p, d + 1)
-    z_down = remote(edge.at[0], side_z.at[1], z_send.at[1], z_recv.at[1], p, d - 1)
-    has_below, has_above = p > 0, p < planes - 1
-    has_front, has_back = d > 0, d < depths - 1
-    pl.when(has_above)(x_up.start)
-    pl.when(has_below)(x_down.start)
+    lax.fori_loop(0, cells_x, turn, 0, unroll=True)
+
     pl.when(has_back)(z_up.start)
     pl.when(has_front)(z_down.start)
 
     def resampled(field, first, count):
-        for x in range(first, first + count):
-            samples[field, x] = lax.dot_general(
-                fields[field, x], mat[...], (((1,), (1,)), ((), ())),
-                preferred_element_type=jnp.float32,
-            )
+        block = fields[field, first : first + count].reshape(count * cells_z, cells_y)
+        found = lax.dot_general(
+            block, mat[...], (((1,), (1,)), ((), ())), preferred_element_type=jnp.float32
+        )
+        samples[field, first : first + count] = found.reshape(count, cells_z, cells_y)
 
     loads[cells_x].wait()
     resampled(0, 0, cells_x)
@@ -116,7 +115,7 @@
         ).astype(jnp.bfloat16)
         return carry
 
-    lax.fori_loop(0, cells_x * cells_x, slope_y, 0)
+    lax.fori_loop(0, cells_x * cells_x, slope_y, 0, unroll=True)
     resampled(2, 0, cells_x)
 
     loads[cells_x + 1].wait()
@@ -158,18 +157,19 @@
                 tint[channel, x, at, here] = looked_up(channel)
         return carry
 
-    lax.fori_loop(0, cells_x * cells_x, density, 0)
+    lax.fori_loop(0, cells_x * cells_x, density, 0, unroll=True)
 
     row = lax.broadcasted_iota(jnp.int32, (cells_z, cells_z), 0)
     column = lax.broadcasted_iota(jnp.int32, (cells_z, cells_z), 1)
     earlier = jnp.where((column < row) & (column // group == row // group), 1.0, 0.0)
     earlier = earlier.astype(jnp.bfloat16)
+    earlier = jnp.concatenate([earlier, earlier], axis=1)
     for x in range(cells_x):
         tau = taus[x]
         high = tau.astype(jnp.bfloat16)
         low = (tau - high.astype(jnp.float32)).astype(jnp.bfloat16)
-        before[x] = jnp.dot(earlier, high, preferred_element_type=jnp.float32) + jnp.dot(
-            earlier, low, preferred_element_type=jnp.float32
+        before[x] = jnp.dot(
+            earlier, jnp.concatenate([high, low], axis=0), preferred_element_type=jnp.float32
         )
 
     pl.when(has_front)(z_down.wait_send)
@@ -194,42 +194,14 @@
         fields[3, x] = ((ahead - behind) * 0.5).astype(jnp.bfloat16)
     resampled(3, 0, cells_x)
 
-    def slope_x(x, carry):
-        ahead = tall[x + 2, PAD : PAD + cells_z]
-        behind = tall[x, PAD : PAD + cells_z]
-        fields[1, x] = ((ahead - behind) * 0.5).astype(jnp.bfloat16)
-        return carry
-
-    lax.fori_loop(1, cells_x - 1, slope_x, 0)
-    resampled(1, 1, cells_x - 2)
-    pl.when(has_above)(x_up.wait_send)
-    pl.when(has_below)(x_down.wait_send)
-    pl.when(has_below)(x_up.wait_recv)
-    pl.when(has_above)(x_down.wait_recv)
-
-    @pl.when(jnp.logical_not(has_below))
-    def _():
-        side_x[0] = jnp.zeros_like(side_x[0])
-
-    @pl.when(jnp.logical_not(has_above))
-    def _():
-        side_x[1] = jnp.zeros_like(side_x[1])
-
-    tall[0, PAD : PAD + cells_z] = side_x[0].T
-    tall[cells_x + 1, PAD : PAD + cells_z] = side_x[1].T
-    slope_x(0, 0)
-    slope_x(cells_x - 1, 0)
-    resampled(1, 0, 1)
-    resampled(1, cells_x - 1, 1)
-
     light_x, light_y, light_z = light[0], light[1], light[2]
 
-    def composite(step, carry):
-        x, part = step // cells_x, step % cells_x
+    def composite(first, step, carry):
+        x, part = first + step // cells_x, step % cells_x
         at = pl.ds(pl.multiple_of(part * group, 16), group)
         for tile in range(cells_y // lanes):
             here = slice(tile * lanes, (tile + 1) * lanes)
-            grad_x = samples[1, x, at, here]
+            grad_x = samples[1, (x - 1) % cells_x, at, here]
             grad_y = samples[2, x, at, here]
             grad_z = samples[3, x, at, here]
             lit = jnp.abs(grad_x * light_x + grad_y * light_y + grad_z * light_z)
@@ -244,7 +216,40 @@
             pieces[part, 3, x, :, here] = jnp.sum(tau, axis=0, keepdims=True)
         return carry
 
-    lax.fori_loop(0, cells_x * cells_x, composite, 0)
+    def composited(first, count):
+        lax.fori_loop(
+            0, count * cells_x, functools.partial(composite, first), 0, unroll=True
+        )
+
+    def slope_x(x):
+        ahead = tall[x + 2, PAD : PAD + cells_z]
+        behind = tall[x, PAD : PAD + cells_z]
+        fields[1, (x - 1) % cells_x] = ((ahead - behind) * 0.5).astype(jnp.bfloat16)
+
+    for x in range(1, cells_x - 1):
+        slope_x(x)
+    resampled(1, 0, cells_x - 2)
+    composited(1, cells_x - 2)
+    pl.when(has_above)(x_up.wait_send)
+    pl.when(has_below)(x_down.wait_send)
+    pl.when(has_below)(x_up.wait_recv)
+    pl.when(has_above)(x_down.wait_recv)
+
+    @pl.when(jnp.logical_not(has_below))
+    def _():
+        side_x[0] = jnp.zeros_like(side_x[0])
+
+    @pl.when(jnp.logical_not(has_above))
+    def _():
+        side_x[1] = jnp.zeros_like(side_x[1])
+
+    tall[0, PAD : PAD + cells_z] = side_x[0].T
+    tall[cells_x + 1, PAD : PAD + cells_z] = side_x[1].T
+    slope_x(0)
+    slope_x(cells_x - 1)
+    resampled(1, cells_x - 2, 2)
+    composited(0, 1)
+    composited(cells_x - 1, 1)
 
     def placed(part, channel):
         ahead = [jnp.zeros((part, cells_y), jnp.float32)] if part else []
@@ -330,9 +335,9 @@
         functools.partial(kernel, planes, depths),
         out_shape=jax.ShapeDtypeStruct((4, cells_x, share), f32),
         in_specs=[
-            pl.BlockSpec(memory_space=pl.ANY),
-            pl.BlockSpec(memory_space=pl.ANY),
-            pl.BlockSpec(memory_space=pl.ANY),
+            pl.BlockSpec(memory_space=pltpu.HBM),
+            pl.BlockSpec(memory_space=pltpu.HBM),
+            pl.BlockSpec(memory_space=pltpu.HBM),
             pl.BlockSpec(memory_space=pltpu.VMEM),
             pl.BlockSpec(memory_space=pltpu.SMEM),
         ],
@@ -352,7 +357,7 @@
             pltpu.VMEM((cells_x, cells_z, cells_y), f32),
             pltpu.VMEM((3, cells_x, cells_z, cells_y), f32),
             pltpu.VMEM((cells_x, 4, cells_x, 1, cells_y), f32),
-            pltpu.VMEM((128, 128), f32),
+            pltpu.VMEM((16, 128), f32),
             pltpu.VMEM((2, depths, 4, cells_x, share), f32),
             pltpu.VMEM((depths, 2, 4, cells_x, share), f32),
             dma((cells_x + 2,)),
@@ -366,7 +371,7 @@
         compiler_params=pltpu.CompilerParams(
             collective_id=0, has_side_effects=True, vmem_limit_bytes=40 * 1024 * 1024
         ),
-    )(volume, resample, ray_bounds, transfer, light)
+    )(volume, resample, ray_bounds, transfer.T, light)
 
 
 def solution(mesh):

time: 25.8 us -> 21.3 us (0.83)
  Pallas kernels: 21 us -> 15.9 us
  local copies, waits for them, and re-layouts: 4.6 us -> 5.16 us
    pallas_call x1, Pallas kernels: 21 us -> 15.9 us  [body(): pl.pallas_call(functools.partial(kernel, planes, depths), out_shape=jax.S...]
    unnamed x10 -> x11, local copies, waits for them, and re-layouts: 4.6 us -> 5.16 us
where the time goes in v2:
time: 21.3 us; the launch traced here: 21 us
  Pallas kernels  15.9 us (75%)
  local copies, waits for them, and re-layouts  5.16 us (24%)
    pallas_call x1, Pallas kernels, body(): pl.pallas_call(functools.partial(kernel, planes, depths), out_shape=jax.S...  15.9 us
    unnamed x11, local copies, waits for them, and re-layouts  5.16 us

profile of v2, /device:TPU:16, one launch (start us, length us, event | category | flops | bytes accessed | tf_op | source)
XLA Modules:
  0.0 21.0 jit_solution(9196049014858471292)
XLA Ops:
  0.0 0.0 copy-start.4
  0.0 0.7 %copy-done.4 = f32[3]{0:T(128)S(1)} copy-done((f32[3]{0:T(128)S(1)}, f32[3]{0:T(128)}, u32[]{:S(2)}) %copy-start.4) | copy-done | bytes 36
  0.7 0.0 copy-start
  0.7 1.2 %copy-done = f32[4,512,128]{2,1,0:T(8,128)S(1)} copy-done((f32[4,512,128]{2,1,0:T(8,128)S(1)}, f32[4,512,128]{2,1,0:T(8,128)}, u32[]{:S(2)}) %copy-start) | copy-done | bytes 1048600
  1.9 0.0 copy-start.1
  1.9 1.0 %copy-done.1 = bf16[512,512]{1,0:T(8,128)(2,1)S(1)} copy-done((bf16[512,512]{1,0:T(8,128)(2,1)S(1)}, bf16[512,512]{1,0:T(8,128)(2,1)}, u32[]{:S(2)}) %copy-start.1) | copy-done | bytes 524312
  2.9 0.0 copy-start.2
  2.9 0.9 %copy-done.2 = s32[2,64,512]{2,1,0:T(8,128)S(1)} copy-done((s32[2,64,512]{2,1,0:T(8,128)S(1)}, s32[2,64,512]{2,1,0:T(8,128)}, u32[]{:S(2)}) %copy-start.2) | copy-done | bytes 262168
  3.9 0.0 copy-start.3
  3.9 0.7 %copy-done.3 = f32[16,4]{0,1:T(4,128)S(1)} copy-done((f32[16,4]{0,1:T(4,128)S(1)}, f32[16,4]{0,1:T(4,128)}, u32[]{:S(2)}) %copy-start.3) | copy-done | bytes 280
  4.6 15.9 %shard_map.55 = f32[4,4,256]{2,1,0:T(4,128)S(1)} custom-call(f32[4,512,128]{2,1,0:T(8,128)S(1)} %copy-done, bf16[512,512]{1,0:T(8,128)(2,1)S(1)} %copy-done.1, s32[2,64,512]{2,1,0:T(8,128)S(1)} %copy-done.2, f32[4,16]{1,0:T(4,128)S(1)} %bitcast.1, f32[3]{0:T(128)S(1)} %copy-done.4), custom_call_target="tpu_custom_call" | custom-call | tf_op jit(solution)/shard_map/pallas_call | solution.py:334
  20.4 0.6 %copy.7 = f32[4,4,256]{2,1,0:T(4,128)} copy(f32[4,4,256]{2,1,0:T(4,128)S(1)} %shard_map.55) | data formatting | bytes 32768
Async XLA Ops:
  0.0 0.7 %copy-start.4 = (f32[3]{0:T(128)S(1)}, f32[3]{0:T(128)}, u32[]{:S(2)}) copy-start(f32[3]{0:T(128)} %light.1) | copy-start | bytes 40
  0.7 1.2 %copy-start = (f32[4,512,128]{2,1,0:T(8,128)S(1)}, f32[4,512,128]{2,1,0:T(8,128)}, u32[]{:S(2)}) copy-start(f32[4,512,128]{2,1,0:T(8,128)} %volume.1) | copy-start | bytes 3145732
  1.9 1.0 %copy-start.1 = (bf16[512,512]{1,0:T(8,128)(2,1)S(1)}, bf16[512,512]{1,0:T(8,128)(2,1)}, u32[]{:S(2)}) copy-start(bf16[512,512]{1,0:T(8,128)(2,1)} %resample.1) | copy-start | bytes 1572868
  2.9 0.9 %copy-start.2 = (s32[2,64,512]{2,1,0:T(8,128)S(1)}, s32[2,64,512]{2,1,0:T(8,128)}, u32[]{:S(2)}) copy-start(s32[2,64,512]{2,1,0:T(8,128)} %bounds.1) | copy-start | bytes 786436
  3.9 0.7 %copy-start.3 = (f32[16,4]{0,1:T(4,128)S(1)}, f32[16,4]{0,1:T(4,128)}, u32[]{:S(2)}) copy-start(f32[16,4]{0,1:T(4,128)} %param.7) | copy-start | bytes 772

commit v3 on v2

--- a/solution.py
+++ b/solution.py
@@ -196,30 +196,31 @@
 
     light_x, light_y, light_z = light[0], light[1], light[2]
 
-    def composite(first, step, carry):
-        x, part = first + step // cells_x, step % cells_x
-        at = pl.ds(pl.multiple_of(part * group, 16), group)
-        for tile in range(cells_y // lanes):
-            here = slice(tile * lanes, (tile + 1) * lanes)
-            grad_x = samples[1, (x - 1) % cells_x, at, here]
-            grad_y = samples[2, x, at, here]
-            grad_z = samples[3, x, at, here]
-            lit = jnp.abs(grad_x * light_x + grad_y * light_y + grad_z * light_z)
-            norm = grad_x * grad_x + grad_y * grad_y + grad_z * grad_z + 1.0
-            lit = 0.3 + 0.7 * lit * lax.rsqrt(norm)
-            tau = taus[x, at, here]
-            weight = jnp.exp(-before[x, at, here]) * (1.0 - jnp.exp(-tau)) * lit
-            for channel in range(3):
-                pieces[part, channel, x, :, here] = jnp.sum(
-                    weight * tint[channel, x, at, here], axis=0, keepdims=True
-                )
-            pieces[part, 3, x, :, here] = jnp.sum(tau, axis=0, keepdims=True)
-        return carry
-
-    def composited(first, count):
-        lax.fori_loop(
-            0, count * cells_x, functools.partial(composite, first), 0, unroll=True
-        )
+    def tiles(first, count):
+        for x in range(first, first + count):
+            for part in range(cells_x):
+                for tile in range(cells_y // lanes):
+                    at = slice(part * group, (part + 1) * group)
+                    yield x, part, at, slice(tile * lanes, (tile + 1) * lanes)
+
+    def prepared(x, part, at, here):
+        grad_y = samples[2, x, at, here]
+        grad_z = samples[3, x, at, here]
+        along = grad_y * light_y + grad_z * light_z
+        norm = grad_y * grad_y + grad_z * grad_z + 1.0
+        tau = taus[x, at, here]
+        ahead = before[x, at, here]
+        pieces[part, 3, x, :, here] = ahead[group - 1 :] + tau[group - 1 :]
+        return along, norm, jnp.exp(-ahead) * (1.0 - jnp.exp(-tau))
+
+    def finished(x, part, at, here, along, norm, weight):
+        grad_x = samples[1, (x - 1) % cells_x, at, here]
+        lit = 0.7 * jnp.abs(along + grad_x * light_x) * lax.rsqrt(norm + grad_x * grad_x)
+        weight = weight * (lit + 0.3)
+        for channel in range(3):
+            pieces[part, channel, x, :, here] = jnp.sum(
+                weight * tint[channel, x, at, here], axis=0, keepdims=True
+            )
 
     def slope_x(x):
         ahead = tall[x + 2, PAD : PAD + cells_z]
@@ -229,7 +230,15 @@
     for x in range(1, cells_x - 1):
         slope_x(x)
     resampled(1, 0, cells_x - 2)
-    composited(1, cells_x - 2)
+    for place in tiles(1, cells_x - 2):
+        finished(*place, *prepared(*place))
+    for edge_x in (0, cells_x - 1):
+        for place in tiles(edge_x, 1):
+            x, part, at, here = place
+            along, norm, weight = prepared(*place)
+            samples[2, x, at, here] = along
+            samples[3, x, at, here] = norm
+            before[x, at, here] = weight
     pl.when(has_above)(x_up.wait_send)
     pl.when(has_below)(x_down.wait_send)
     pl.when(has_below)(x_up.wait_recv)
@@ -248,8 +257,12 @@
     slope_x(0)
     slope_x(cells_x - 1)
     resampled(1, cells_x - 2, 2)
-    composited(0, 1)
-    composited(cells_x - 1, 1)
+    for edge_x in (0, cells_x - 1):
+        for place in tiles(edge_x, 1):
+            x, part, at, here = place
+            finished(
+                *place, samples[2, x, at, here], samples[3, x, at, here], before[x, at, here]
+            )
 
     def placed(part, channel):
         ahead = [jnp.zeros((part, cells_y), jnp.float32)] if part else []
@@ -369,7 +382,7 @@
             dma((depths, 2)),
         ],
         compiler_params=pltpu.CompilerParams(
-            collective_id=0, has_side_effects=True, vmem_limit_bytes=40 * 1024 * 1024
+            collective_id=0, has_side_effects=True, vmem_limit_bytes=64 * 1024 * 1024
         ),
     )(volume, resample, ray_bounds, transfer.T, light)
 

time: 21.3 us -> 18.1 us (0.85)
  local copies, waits for them, and re-layouts: 5.16 us -> 1.32 us
  Pallas kernels: 15.9 us -> 16.5 us
    unnamed x11 -> x1, local copies, waits for them, and re-layouts: 5.16 us -> 1.32 us
    pallas_call x1, Pallas kernels: 15.9 us -> 16.5 us  [body(): pl.pallas_call(functools.partial(kernel, planes, depths), out_shape=jax.S...]
where the time goes in v3:
time: 18.1 us; the launch traced here: 17.9 us
  Pallas kernels  16.5 us (91%)
  local copies, waits for them, and re-layouts  1.32 us (7%)
    pallas_call x1, Pallas kernels, body(): pl.pallas_call(functools.partial(kernel, planes, depths), out_shape=jax.S...  16.5 us
    unnamed x1, local copies, waits for them, and re-layouts  1.32 us

profile of v3, /device:TPU:16, one launch (start us, length us, event | category | flops | bytes accessed | tf_op | source)
XLA Modules:
  0.0 17.9 jit_solution(10008271184228351301)
XLA Ops:
  0.0 16.5 %shard_map.55 = f32[4,4,256]{2,1,0:T(4,128)} custom-call(f32[4,512,128]{2,1,0:T(8,128)} %volume.1, bf16[512,512]{1,0:T(8,128)(2,1)} %resample.1, s32[2,64,512]{2,1,0:T(8,128)} %bounds.1, f32[4,16]{1,0:T(4,128)} %bitcast.1, f32[3]{0:T(128)} %light.1), custom_call_target="tpu_custom_call" | custom-call | tf_op jit(solution)/shard_map/pallas_call | solution.py:347
  16.6 1.3 %copy.7 = f32[4,4,256]{2,1,0:T(4,128)} copy(f32[4,4,256]{2,1,0:T(4,128)} %shard_map.55) | data formatting | bytes 32768

commit v4 on v3

--- a/solution.py
+++ b/solution.py
@@ -9,6 +9,18 @@
 
 MESH = pl.DeviceIdType.MESH
 PAD = 8
+VMEM_BYTES = 64 * 1024 * 1024
+
+
+def at_knots(row, knot):
+    numbers = lax.GatherDimensionNumbers(
+        offset_dims=(), collapsed_slice_dims=(1,), start_index_map=(1,),
+        operand_batching_dims=(0,), start_indices_batching_dims=(0,),
+    )
+    return lax.gather(
+        row, knot[:, :, None], numbers, slice_sizes=(1, 1),
+        mode=lax.GatherScatterMode.PROMISE_IN_BOUNDS,
+    )
 
 
 def kernel(
@@ -50,7 +62,9 @@
         greet(p - source - 1 >= 0, p - source - 1, source)
 
     table[...] = jnp.zeros_like(table)
+    step_size = 2.0 / (depths * cells_z)
     table[:channels, :knots] = transfer[...]
+    table[3:4, :knots] = transfer[3:4] * step_size
     flat = table[:8]
     knot_index = lax.broadcasted_iota(jnp.int32, flat.shape, 1)
     slope = jnp.where(knot_index < knots - 1, pltpu.roll(flat, lanes - 1, 1) - flat, 0.0)
@@ -111,7 +125,7 @@
         upper = jnp.where(lane < cells_y - 1, pltpu.roll(block, cells_y - 1, 1), 0.0)
         lower = jnp.where(lane > 0, pltpu.roll(block, 1, 1), 0.0)
         fields[2, x, pl.ds(pl.multiple_of(part * group, 16), group)] = (
-            (upper - lower) * 0.5
+            upper - lower
         ).astype(jnp.bfloat16)
         return carry
 
@@ -130,7 +144,6 @@
             window[end, pixel] = aligned[pixel : pixel + 1]
 
     scale = (knots - 1) / 5.0
-    step_size = 2.0 / (depths * cells_z)
 
     def density(step, carry):
         x, part = step // cells_x, step % cells_x
@@ -145,14 +158,12 @@
             def looked_up(channel):
                 base = jnp.broadcast_to(table[channel : channel + 1], (group, lanes))
                 tilt = jnp.broadcast_to(table[8 + channel : 9 + channel], (group, lanes))
-                return jnp.take_along_axis(
-                    base, knot, axis=1, mode="promise_in_bounds"
-                ) + rest * jnp.take_along_axis(tilt, knot, axis=1, mode="promise_in_bounds")
+                return at_knots(base, knot) + rest * at_knots(tilt, knot)
 
             first = window[0, x + part, :, here]
             last = window[1, x + part, :, here]
             inside = (index >= first) & (index < last)
-            taus[x, at, here] = jnp.where(inside, step_size * looked_up(3), 0.0)
+            taus[x, at, here] = jnp.where(inside, looked_up(3), 0.0)
             for channel in range(3):
                 tint[channel, x, at, here] = looked_up(channel)
         return carry
@@ -191,7 +202,7 @@
     for x in range(cells_x):
         ahead = tall[x + 1, PAD + 1 : PAD + 1 + cells_z]
         behind = tall[x + 1, PAD - 1 : PAD - 1 + cells_z]
-        fields[3, x] = ((ahead - behind) * 0.5).astype(jnp.bfloat16)
+        fields[3, x] = (ahead - behind).astype(jnp.bfloat16)
     resampled(3, 0, cells_x)
 
     light_x, light_y, light_z = light[0], light[1], light[2]
@@ -207,7 +218,7 @@
         grad_y = samples[2, x, at, here]
         grad_z = samples[3, x, at, here]
         along = grad_y * light_y + grad_z * light_z
-        norm = grad_y * grad_y + grad_z * grad_z + 1.0
+        norm = grad_y * grad_y + grad_z * grad_z + 4.0
         tau = taus[x, at, here]
         ahead = before[x, at, here]
         pieces[part, 3, x, :, here] = ahead[group - 1 :] + tau[group - 1 :]
@@ -225,7 +236,7 @@
     def slope_x(x):
         ahead = tall[x + 2, PAD : PAD + cells_z]
         behind = tall[x, PAD : PAD + cells_z]
-        fields[1, (x - 1) % cells_x] = ((ahead - behind) * 0.5).astype(jnp.bfloat16)
+        fields[1, (x - 1) % cells_x] = (ahead - behind).astype(jnp.bfloat16)
 
     for x in range(1, cells_x - 1):
         slope_x(x)
@@ -342,6 +353,7 @@
     planes = lax.axis_size("plane")
     depths = lax.axis_size("depth")
     share = cells_y // depths
+    room = 4 * cells_x * share * 4
     f32 = jnp.float32
     dma = pltpu.SemaphoreType.DMA
     return pl.pallas_call(
@@ -382,7 +394,7 @@
             dma((depths, 2)),
         ],
         compiler_params=pltpu.CompilerParams(
-            collective_id=0, has_side_effects=True, vmem_limit_bytes=64 * 1024 * 1024
+            collective_id=0, has_side_effects=True, vmem_limit_bytes=VMEM_BYTES - room
         ),
     )(volume, resample, ray_bounds, transfer.T, light)
 

time: 18.1 us -> 18.1 us (level)
  no operation moved by 1% of the time
where the time goes in v4:
time: 18.1 us; the launch traced here: 17.8 us
  Pallas kernels  16.5 us (91%)
  local copies, waits for them, and re-layouts  1.32 us (7%)
    pallas_call x1, Pallas kernels, body(): pl.pallas_call(functools.partial(kernel, planes, depths), out_shape=jax.S...  16.5 us
    unnamed x1, local copies, waits for them, and re-layouts  1.32 us

profile of v4, /device:TPU:16, one launch (start us, length us, event | category | flops | bytes accessed | tf_op | source)
XLA Modules:
  0.0 17.8 jit_solution(378550049462775198)
XLA Ops:
  0.0 16.5 %shard_map.55 = f32[4,4,256]{2,1,0:T(4,128)} custom-call(f32[4,512,128]{2,1,0:T(8,128)} %volume.1, bf16[512,512]{1,0:T(8,128)(2,1)} %resample.1, s32[2,64,512]{2,1,0:T(8,128)} %bounds.1, f32[4,16]{1,0:T(4,128)} %bitcast.1, f32[3]{0:T(128)} %light.1), custom_call_target="tpu_custom_call" | custom-call | tf_op jit(solution)/shard_map/pallas_call | solution.py:359
  16.5 1.3 %copy.7 = f32[4,4,256]{2,1,0:T(4,128)} copy(f32[4,4,256]{2,1,0:T(4,128)} %shard_map.55) | data formatting | bytes 32768

commit v5 on v4

--- a/solution.py
+++ b/solution.py
@@ -111,11 +111,12 @@
     def resampled(field, first, count):
         block = fields[field, first : first + count].reshape(count * cells_z, cells_y)
         found = lax.dot_general(
-            block, mat[...], (((1,), (1,)), ((), ())), preferred_element_type=jnp.float32
+            block, mat[...], (((1,), (0,)), ((), ())), preferred_element_type=jnp.float32
         )
         samples[field, first : first + count] = found.reshape(count, cells_z, cells_y)
 
     loads[cells_x].wait()
+    mat[...] = mat[...].T
     resampled(0, 0, cells_x)
 
     def slope_y(step, carry):

time: 18.1 us -> 18.2 us (level)
  no operation moved by 1% of the time
where the time goes in v5:
time: 18.2 us; the launch traced here: 18 us
  Pallas kernels  16.6 us (91%)
  local copies, waits for them, and re-layouts  1.32 us (7%)
    pallas_call x1, Pallas kernels, body(): pl.pallas_call(functools.partial(kernel, planes, depths), out_shape=jax.S...  16.6 us
    unnamed x1, local copies, waits for them, and re-layouts  1.32 us

profile of v5, /device:TPU:16, one launch (start us, length us, event | category | flops | bytes accessed | tf_op | source)
XLA Modules:
  0.0 18.0 jit_solution(16838367700443618648)
XLA Ops:
  0.0 16.6 %shard_map.55 = f32[4,4,256]{2,1,0:T(4,128)} custom-call(f32[4,512,128]{2,1,0:T(8,128)} %volume.1, bf16[512,512]{1,0:T(8,128)(2,1)} %resample.1, s32[2,64,512]{2,1,0:T(8,128)} %bounds.1, f32[4,16]{1,0:T(4,128)} %bitcast.1, f32[3]{0:T(128)} %light.1), custom_call_target="tpu_custom_call" | custom-call | tf_op jit(solution)/shard_map/pallas_call | solution.py:360
  16.6 1.3 %copy.7 = f32[4,4,256]{2,1,0:T(4,128)} copy(f32[4,4,256]{2,1,0:T(4,128)} %shard_map.55) | data formatting | bytes 32768
